TPU v7x, 512 devices: a whole 4x8x8 slice. The times are simulated.
512 devices in a mesh: val: 16 (over x, y_hi, core), cond: 32 (over z, y_lo).
Axes of the slice: x: 4, y: 8 (y_hi: 2, y_lo: 4; y = y_hi * 4 + y_lo), z: 8, core: 2. Of those that a mesh axis runs over, the one named last changes fastest.
Arguments:
- val_orbitals: bfloat16 [64, 768], P('val'), may hold values from -6 to 6
- cond_orbitals: bfloat16 [256, 768], P('cond'), may hold values from -6 to 6
- val_energy: bfloat16 [64], P('val'), may hold values from -0.59765625 to -0.049804688
- cond_energy: bfloat16 [256], P('cond'), may hold values from 0.049804688 to 1.1953125
- wave_index: int32 [4096], P('cond'), may hold values from 0 to 884735
Outputs:
- chi_real: float32 [128, 4096], P('val', 'cond')
- chi_imag: float32 [128, 4096], P('val', 'cond')
Inputs may be any that keep to these rules, and one draw needn't show every extreme that they name: `wave_index`: values may repeat.
All inputs are finite; a program needn't handle non-finite values.
Results may differ from a plain program's by a relative error of at most 0.0037.
Values may be sent and summed in bfloat16 or wider, within the bound.
No kernel may reach another device: no remote copies, remote signals or barrier semaphores. Data moves between devices by JAX's collectives and lax.ppermute only.
A program may use at most 64 MiB of HBM per device.

v0:
```python
import math

import jax
import jax.numpy as jnp
from jax import lax
from jax.sharding import PartitionSpec as P

NG = 96
NW = 128
VB = 4
CB = 8
SLAB_Y = 4
NPTS = 768


def picked(value, axis, root):
    return lax.dynamic_index_in_dim(lax.all_gather(value, axis), root, 0, keepdims=False)


def from_everyone(value, axis):
    copies = jnp.broadcast_to(value, (lax.axis_size(axis), *value.shape))
    return lax.all_to_all(copies, axis, split_axis=0, concat_axis=0, tiled=True)


def laid_out(pieces, dim):
    pieces = jnp.moveaxis(pieces, 0, dim)
    lengths = pieces.shape
    return pieces.reshape(*lengths[:dim], lengths[dim] * lengths[dim + 1], *lengths[dim + 2 :])


def collect(value, axis, dim):
    pieces = from_everyone(value, axis)
    return laid_out(pieces, dim)


def sent_together(arrays, axis, dim, along):
    widths = [math.prod(a.shape[along:]) for a in arrays]
    both = jnp.concatenate(
        [a.reshape(*a.shape[:along], w) for a, w in zip(arrays, widths)], axis=along
    )
    whole = collect(both, axis, dim)
    pieces = jnp.split(whole, [sum(widths[:k]) for k in range(1, len(widths))], axis=along)
    return tuple(
        (b.reshape(*whole.shape[:along], *a.shape[along:]) for a, b in zip(arrays, pieces))
    )


def cut_along(value, dim, length):
    lengths = value.shape
    pieces = value.reshape(*lengths[:dim], length, lengths[dim] // length, *lengths[dim + 1 :])
    return jnp.moveaxis(pieces, dim, 0)


def summed_on_arrival(value, axis, dim):
    length = lax.axis_size(axis)
    pieces = lax.all_to_all(cut_along(value, dim, length), axis, 0, 0, tiled=True)
    return jnp.sum(pieces, axis=0)


def side_by_side(arrays, axis, dim, along):
    ends, at = ([], 0)
    for a in arrays[:-1]:
        at += a.shape[along]
        ends.append(at)
    both = jnp.concatenate(arrays, axis=along)
    return tuple(jnp.split(summed_on_arrival(both, axis, dim), ends, axis=along))


def phase_table(wave_index, point_count, grid_cells, slab_rows):
    points = lax.iota(jnp.int32, point_count)
    along_x = points % grid_cells
    along_y = points // grid_cells % slab_rows
    along_z = points // (grid_cells * slab_rows)
    wave_x = wave_index // (grid_cells * grid_cells)
    wave_y = wave_index // grid_cells % grid_cells
    wave_z = wave_index % grid_cells
    phase_turns = (
        along_x[:, None] * wave_x[None, :]
        + along_y[:, None] * wave_y[None, :]
        + along_z[:, None] * wave_z[None, :]
    ) % grid_cells
    angles = phase_turns.astype(jnp.float32) * (2.0 * math.pi / grid_cells)
    return jnp.concatenate([jnp.cos(angles), jnp.sin(angles)], axis=1).astype(jnp.bfloat16)


def pair_density(valence, conduction):
    product = conduction[:, None, :].astype(jnp.float32) * valence[None, :, :].astype(jnp.float32)
    return product.reshape(-1, valence.shape[1]).astype(jnp.bfloat16)


def pair_weights(val_energy, cond_energy):
    spread = cond_energy[:, None].astype(jnp.float32) - val_energy[None, :].astype(jnp.float32)
    return (1.0 / spread).reshape(-1)


def per_device(val_orbitals, cond_orbitals, val_energy, cond_energy, wave_index):
    window_index = picked(wave_index, "cond", 0)
    row_table = phase_table(wave_index, NPTS, NG, SLAB_Y)
    window_table = phase_table(window_index, NPTS, NG, SLAB_Y)
    row_count = wave_index.shape[0]
    factor = -4.0 / math.sqrt(VB * lax.axis_size("val") * CB * lax.axis_size("cond"))
    conduction, energy = sent_together((cond_orbitals, cond_energy), "cond", 0, 1)
    density = pair_density(val_orbitals, conduction)
    weights = pair_weights(val_energy, energy)
    window_terms = jnp.dot(density, window_table, preferred_element_type=jnp.float32)
    weighted = window_terms * weights[:, None]
    row_terms = jnp.dot(density, row_table, preferred_element_type=jnp.float32)
    update = jnp.dot(weighted.T, row_terms, precision=lax.Precision.HIGHEST)
    real_part = factor * (update[:NW, :row_count] + update[NW:, row_count:])
    imag_part = factor * (update[:NW, row_count:] - update[NW:, :row_count])
    return side_by_side((real_part, imag_part), "val", 0, 1)


def solution(mesh):
    return jax.shard_map(
        per_device,
        mesh=mesh,
        in_specs=(P("val", None), P("cond", None), P("val"), P("cond"), P("cond")),
        out_specs=(P("val", "cond"), P("val", "cond")),
        check_vma=False,
    )
```

profile of v0, /device:TPU:1, one launch (start us, length us, event | category | flops | bytes accessed | tf_op | source)
XLA Modules:
  0.0 125.5 jit_solution(6039692616600960632)
XLA Ops:
  0.6 0.7 copy.14
  1.4 0.7 pad_maximum_fusion.1
  2.1 0.8 broadcast_in_dim.2
  2.9 14.3 %all-to-all-start = ((bf16[32,8,769]{2,1,0:T(8,128)(2,1)}), bf16[32,8,769]{2,1,0:T(8,128)(2,1)S(1)}, u32[]{:S(2)}, u32[]{:S(2)}) async-start(bf16[32,8,769]{2,1,0:T(8,128)(2,1)} %broadcast_in_dim.2), calls=%async_computation | async-start | bytes 917504 | tf_op jit(solution)/shard_map/all_to_all | solution.py:22
  17.2 0.7 convert_element_type.32
  17.9 0.7 convert_element_type.28
  18.6 64.4 %all-gather.1 = s32[32,1,128]{2,1,0:T(1,128)S(1)} all-gather(s32[1,1,128]{2,1,0:T(1,128)} %bitcast.45), channel_id=2, replica_groups=mesh['val'=16,'cond'=32] {'cond'}, dimensions={0}, use_global_device_ids=true | all-gather | bytes 16896 | tf_op jit(solution)/shard_map/all_gather | solution.py:17
  83.0 0.7 and_select_fusion.3
  83.7 4.7 %cosine_convert_fusion = (bf16[768,128]{1,0:T(8,128)(2,1)S(1)}, bf16[768,128]{1,0:T(8,128)(2,1)S(1)}, bf16[768,128]{1,0:T(8,128)(2,1)}, bf16[768,128]{1,0:T(8,128)(2,1)}) fusion(s32[128]{0:T(128)S(1)} %get-tuple-element.17, s32[768]{0:T(1024)S(1)} %get-tuple-element.18, s32[128]{0:T(128)S(1)} %get-tuple-element.16, s32[768]{0:T(1024)S(1)} %get-tuple-element.19, ...), kind=kLoop, calls=%fused_computation.17 | loop fusion | flops 2949120 | bytes 798720 | tf_op jit(solution)/shard_map/convert.1
  88.4 0.0 all-to-all-done
  88.4 0.1 convert_reduce_fusion
  88.5 0.1 slice_convert_fusion
  88.6 0.1 subtract_divide_fusion
  88.7 0.1 div.65
  88.8 0.5 multiply_convert_fusion
  89.4 0.4 convert_element_type.30
  89.8 0.0 copy-start
  89.8 0.0 copy-start.1
  89.8 0.6 fusion.7
  90.4 0.3 copy-done
  90.7 0.1 copy-done.1
  90.8 0.6 convolution_multiply_fusion
  91.4 1.8 %fusion.35 = f32[256,256]{0,1:T(8,128)S(1)} fusion(f32[1024,256]{1,0:T(8,128)S(1)} %convolution_multiply_fusion, f32[1024,256]{1,0:T(8,128)S(1)} %fusion.7), kind=kOutput, calls=%fused_computation.71 | convolution fusion | flops 805306368 | bytes 2359296 | tf_op jit(solution)/shard_map/dot_general | solution.py:108
  93.3 0.1 copy.15
  93.4 31.6 %all_to_all.10 = f32[16,8,256]{2,1,0:T(8,128)S(1)} all-to-all(f32[16,8,256]{2,1,0:T(8,128)S(1)} %bitcast.44), channel_id=1, replica_groups=mesh['val'=16,'cond'=32] {'val'}, dimensions={0} | all-to-all | bytes 262144 | tf_op jit(solution)/shard_map/all_to_all | solution.py:56
  124.9 0.6 fusion.34
  (6 shorter events, 0.1 us)
Async XLA Ops:
  2.9 85.5 %all-to-all-start = ((bf16[32,8,769]{2,1,0:T(8,128)(2,1)}), bf16[32,8,769]{2,1,0:T(8,128)(2,1)S(1)}, u32[]{:S(2)}, u32[]{:S(2)}) async-start(bf16[32,8,769]{2,1,0:T(8,128)(2,1)} %broadcast_in_dim.2), calls=%async_computation | async-start | bytes 917504 | tf_op jit(solution)/shard_map/all_to_all | solution.py:22
  89.8 0.9 copy-start
  89.8 1.0 copy-start.1
where the time goes:
time: 126 us
  blocking collectives  96 us (76%)
  starting transfers between devices  14.3 us (11%)
  other arithmetic  8.35 us (7%)
  local copies, waits for them, and re-layouts  3.18 us (3%)
  matrix products  2.97 us (2%)
    all_gather x1, blocking collectives, picked(): lax.all_gather(value, axis)  64.4 us
    all_to_all x1, blocking collectives, summed_on_arrival(): lax.all_to_all(cut_along(value, dim, length), axis, 0, 0, tiled=True)  31.6 us
    all_to_all x1, starting transfers between devices, from_everyone(): return lax.all_to_all(copies, axis, split_axis=0, concat_axis=0, tiled=True)  14.3 us
    another operation x1, other arithmetic  4.7 us
  transfers between devices with their start and end apart: 1, of which 0 were waited for; matrix products, arithmetic and copies ran while one was open for 5% of the time, Pallas kernels for 0%

commit v1 on v0

v1 whole, which is shorter than its diff:
```python
import functools
import math

import jax
import jax.numpy as jnp
from jax import lax
from jax.experimental import pallas as pl
from jax.experimental.pallas import tpu as pltpu
from jax.sharding import PartitionSpec as P

NG = 96
SLAB_Y = 4
NPTS = 768
VMEM = pl.BlockSpec(memory_space=pltpu.VMEM)


def device_number(x, y, z, core):
    val = x * 4 + (y // 4) * 2 + core
    return val * 32 + z * 4 + y % 4


def groups():
    out = []
    for first_y in (2, 6):
        for x0 in range(4):
            for core0 in range(2):
                members = [
                    device_number((z + x0) % 4, (first_y + t) % 8, z, (core0 + z // 4) % 2)
                    for z in range(8)
                    for t in range(4)
                ]
                out.append(sorted(members, key=lambda d: d % 32))
    return out


def whole_part(value, divisor):
    return jnp.floor((value + 0.5) * (1.0 / divisor))


def components(index):
    flat = index.astype(jnp.float32)
    a = whole_part(flat, NG * NG)
    rest = flat - a * (NG * NG)
    b = whole_part(rest, NG)
    return a, b, rest - b * NG


def cos_sin(a, b, c, x, y, z):
    turns = a * x + b * y + c * z
    turns = turns - NG * whole_part(turns, NG)
    angles = turns * (2.0 * math.pi / NG)
    return jnp.cos(angles), jnp.sin(angles)


def grid_points(shape, dim):
    points = lax.broadcasted_iota(jnp.int32, shape, dim).astype(jnp.float32)
    z = whole_part(points, NG * SLAB_Y)
    rest = points - z * (NG * SLAB_Y)
    y = whole_part(rest, NG)
    return rest - y * NG, y, z


def pack_kernel(val_ref, cond_ref, val_energy_ref, cond_energy_ref, index_ref, out_ref):
    odd = lax.rem(lax.axis_index("cond"), 2) == 1
    val = val_ref[...].astype(jnp.float32)
    val = jnp.where(odd, val[2:4], val[0:2])
    a, b, c = components(index_ref[...].reshape(1, 128))
    energy = val_energy_ref[...].astype(jnp.float32)
    energy = jnp.where(odd, energy[:, 2:4], energy[:, 0:2])
    tail = jnp.concatenate(
        [cond_energy_ref[...].astype(jnp.float32), energy, jnp.zeros((1, 118), jnp.float32)], axis=1
    )
    rows = [val[h : h + 1, 256 * q : 256 * q + 256] for h in range(2) for q in range(3)]
    rows += [jnp.concatenate([a, b], axis=1), jnp.concatenate([c, tail], axis=1)]
    side = jnp.concatenate(rows, axis=0)
    block = jnp.concatenate([cond_ref[...].astype(jnp.float32), side], axis=1).astype(jnp.bfloat16)
    for k in range(out_ref.shape[0]):
        out_ref[k] = block


def dot(a, b, dims=(1, 0)):
    return lax.dot_general(
        a, b, (((dims[0],), (dims[1],)), ((), ())), preferred_element_type=jnp.float32
    )


def one_hot(condition):
    return jnp.where(condition, 1.0, 0.0).astype(jnp.bfloat16)


def iotas(rows, cols):
    return (
        lax.broadcasted_iota(jnp.int32, (rows, cols), 0),
        lax.broadcasted_iota(jnp.int32, (rows, cols), 1),
    )


def chi_kernel(factor, got_ref, table_ref, real_ref, imag_ref, left_ref, weighted_ref):
    conduction = got_ref[:, 0:NPTS]
    side = got_ref[:, NPTS:]

    row, lane = iotas(8, 128)
    mine = lane == row + 8 * lax.axis_index("val")
    head = got_ref[0:16, NPTS:].astype(jnp.float32)

    def own(values):
        return jnp.sum(jnp.where(mine, values, 0.0), axis=1, keepdims=True)

    a, b, c = own(head[6:7, 0:128]), own(head[6:7, 128:256]), own(head[7:8, 0:128])
    window = jnp.concatenate(cos_sin(a, b, c, *grid_points((8, NPTS), 1)), axis=0).astype(jnp.bfloat16)
    window = window.astype(jnp.float32)

    v, r = iotas(64, 256)
    first = 8 * (v // 2) + 3 * (v % 2)
    valence = jnp.concatenate([dot(one_hot(r == first + q), side) for q in range(3)], axis=1)
    energies = side[:, 128:256]
    picked = dot(one_hot(r == 8 * (v // 2) + 7), energies)
    v, l = iotas(64, 128)
    val_energy = jnp.sum(jnp.where(l == 8 + v % 2, picked, 0.0), axis=1, keepdims=True)
    r, k = iotas(256, 256)
    spread = dot(energies, one_hot(r == 8 * (k // 8) + 7), (0, 0))
    l, k = iotas(128, 256)
    cond_energy = jnp.sum(jnp.where(l == k % 8, spread, 0.0), axis=0, keepdims=True)
    weights = factor / (cond_energy - val_energy)

    for j in range(16):
        left_ref[64 * j : 64 * j + 64, :] = (valence * window[j : j + 1, :]).astype(jnp.bfloat16)
    terms = dot(left_ref[...], conduction, (1, 1))
    for j in range(16):
        weighted_ref[64 * j : 64 * j + 64, :] = (terms[64 * j : 64 * j + 64, :] * weights).astype(jnp.bfloat16)
    back = dot(weighted_ref[...], conduction)
    totals = jnp.concatenate(
        [jnp.sum(back[64 * j : 64 * j + 64, :] * valence, axis=0, keepdims=True) for j in range(16)], axis=0
    )
    high = totals.astype(jnp.bfloat16)
    low = (totals - high.astype(jnp.float32)).astype(jnp.bfloat16)
    products = dot(high, table_ref[...]) + dot(low, table_ref[...])
    real_ref[...] = products[0:8, 0:128] + products[8:16, 128:256]
    imag_ref[...] = products[0:8, 128:256] - products[8:16, 0:128]


def table_kernel(index_ref, out_ref):
    a, b, c = components(index_ref[...].reshape(1, 128))
    cos, sin = cos_sin(a, b, c, *grid_points((NPTS, 1), 0))
    out_ref[:, 0:128] = cos.astype(jnp.bfloat16)
    out_ref[:, 128:256] = sin.astype(jnp.bfloat16)


def pack(val, cond, val_energy, cond_energy, index):
    return pl.pallas_call(
        pack_kernel,
        out_shape=jax.ShapeDtypeStruct((32, 8, 1024), jnp.bfloat16),
        in_specs=[VMEM] * 5,
        out_specs=VMEM,
    )(val, cond, val_energy, cond_energy, index)


def table(index):
    return pl.pallas_call(
        table_kernel,
        out_shape=jax.ShapeDtypeStruct((NPTS, 256), jnp.bfloat16),
        in_specs=[VMEM],
        out_specs=VMEM,
        cost_estimate=pl.CostEstimate(flops=20_000_000, bytes_accessed=400_000, transcendentals=200_000),
    )(index)


def chi(got, row_table, factor):
    return pl.pallas_call(
        functools.partial(chi_kernel, factor),
        out_shape=[jax.ShapeDtypeStruct((8, 128), jnp.float32)] * 2,
        in_specs=[VMEM] * 2,
        out_specs=[VMEM] * 2,
        scratch_shapes=[pltpu.VMEM((1024, NPTS), jnp.bfloat16), pltpu.VMEM((1024, 256), jnp.bfloat16)],
        compiler_params=pltpu.CompilerParams(vmem_limit_bytes=32 * 1024 * 1024),
    )(got, row_table)


def per_device(val_orbitals, cond_orbitals, val_energy, cond_energy, wave_index):
    factor = -4.0 / math.sqrt(4 * lax.axis_size("val") * 8 * lax.axis_size("cond"))
    sent = pack(
        val_orbitals, cond_orbitals, val_energy.reshape(1, 4), cond_energy.reshape(1, 8), wave_index.reshape(1, 128)
    )
    got = lax.all_to_all(sent, ("val", "cond"), 0, 0, tiled=True, axis_index_groups=groups())
    row_table = table(wave_index.reshape(1, 128))
    return tuple(chi(got.reshape(256, 1024), row_table, factor))


def solution(mesh):
    return jax.shard_map(
        per_device,
        mesh=mesh,
        in_specs=(P("val", None), P("cond", None), P("val"), P("cond"), P("cond")),
        out_specs=(P("val", "cond"), P("val", "cond")),
        check_vma=False,
    )
```

time: 126 us -> 43.6 us (0.35)
  blocking collectives: 96 us -> 0 us
  waiting for transfers between devices: 0.01 us -> 16.2 us
  other arithmetic: 8.35 us -> 0 us
  Pallas kernels: 0 us -> 7.49 us
  starting transfers between devices: 14.3 us -> 18 us
  matrix products: 2.97 us -> 0 us
  local copies, waits for them, and re-layouts: 3.18 us -> 1 us
    all_gather x1 -> x0, blocking collectives: 64.4 us -> none  [picked(): lax.all_gather(value, axis)]
    all_to_all x1 -> x0, blocking collectives: 31.6 us -> none  [summed_on_arrival(): lax.all_to_all(cut_along(value, dim, length), axis, 0, 0, tiled=True)]
    all_to_all x1, waiting for transfers between devices: 0.01 us -> 16.2 us  [per_device(): lax.all_to_all(sent, ('val', 'cond'), 0, 0, tiled=True, axis_index_groups...]
    pallas_call x0 -> x3, Pallas kernels: none -> 7.49 us  [the longest x1 3.13 us: table(): pl.pallas_call(table_kernel, out_shape=jax.ShapeDtypeStruct((NPTS, 256),...]
    another operation x1 -> x0, other arithmetic: 4.7 us -> none
    all_to_all x1, starting transfers between devices: 14.3 us -> 18 us  [per_device(): lax.all_to_all(sent, ('val', 'cond'), 0, 0, tiled=True, axis_index_groups...]
    dot_general x3 -> x0, matrix products: 2.97 us -> none  [the longest x1 1.82 us: per_device(): update = jnp.dot(weighted.T, row_terms, precision=lax.Precision.HIGHEST)]
    convert_element_type x4 -> x0, other arithmetic: 1.96 us -> none  [the longest x1 0.7 us: pair_density(): valence[None, :, :].astype(jnp.float32)]
  transfers between devices with their start and end apart: 1 -> 1, of which waited for: 0 -> 1; matrix products, arithmetic and copies ran while one was open for 5% -> 0% of each run, Pallas kernels for 0% -> 7%
where the time goes in v1:
time: 43.6 us; the launch traced here: 43.3 us
  starting transfers between devices  18 us (41%)
  waiting for transfers between devices  16.2 us (37%)
  Pallas kernels  7.49 us (17%)
  local copies, waits for them, and re-layouts  1 us (2%)
  between operations  0.64 us (1%)
    all_to_all x1, starting transfers between devices, per_device(): lax.all_to_all(sent, ('val', 'cond'), 0, 0, tiled=True, axis_index_groups...  18 us
    all_to_all x1, waiting for transfers between devices, per_device(): lax.all_to_all(sent, ('val', 'cond'), 0, 0, tiled=True, axis_index_groups...  16.2 us
    pallas_call x1, Pallas kernels, table(): pl.pallas_call(table_kernel, out_shape=jax.ShapeDtypeStruct((NPTS, 256),...  3.13 us
    pallas_call x1, Pallas kernels, chi(): pl.pallas_call(functools.partial(chi_kernel, factor), out_shape=[jax.Shap...  2.69 us
    pallas_call x1, Pallas kernels, pack(): pl.pallas_call(pack_kernel, out_shape=jax.ShapeDtypeStruct((32, 8, 1024),...  1.68 us
    unnamed x2, local copies, waits for them, and re-layouts  1 us
  transfers between devices with their start and end apart: 1, of which 1 were waited for; matrix products, arithmetic and copies ran while one was open for 0% of the time, Pallas kernels for 7%

profile of v1, /device:TPU:1, one launch (start us, length us, event | category | flops | bytes accessed | tf_op | source)
XLA Modules:
  0.0 43.3 jit_solution(4091005334468769746)
XLA Ops:
  0.6 1.7 %shard_map.68 = bf16[32,8,1024]{2,1,0:T(8,128)(2,1)} custom-call(bf16[4,768]{1,0:T(4,128)(2,1)} %val_ref.1, bf16[8,768]{1,0:T(8,128)(2,1)} %cond_ref.1, bf16[1,4]{1,0:T(2,128)(2,1)} %bitcast.7, bf16[1,8]{1,0:T(2,128)(2,1)} %bitcast.8, s32[1,128]{1,0:T(1,128)} %bitcast.5), custom_call_target="tpu_custom_call" | custom-call | tf_op jit(solution)/shard_map/pallas_call | solution.py:150
  2.3 18.0 %all-to-all-start = ((bf16[32,8,1024]{2,1,0:T(8,128)(2,1)}), bf16[32,8,1024]{2,1,0:T(8,128)(2,1)S(1)}, u32[]{:S(2)}, u32[]{:S(2)}) async-start(bf16[32,8,1024]{2,1,0:T(8,128)(2,1)} %shard_map.68), calls=%async_computation | async-start | bytes 1048576 | tf_op jit(solution)/shard_map/all_to_all | solution.py:184
  20.3 3.1 %shard_map.69.table_ref = bf16[768,256]{1,0:T(8,128)(2,1)} custom-call(s32[1,128]{1,0:T(1,128)} %bitcast.6), custom_call_target="tpu_custom_call" | custom-call | flops 20000000 | bytes 400000 | tf_op jit(solution)/shard_map/pallas_call | solution.py:159
  23.4 16.2 %all-to-all-done = bf16[32,8,1024]{2,1,0:T(8,128)(2,1)S(1)} async-done(((bf16[32,8,1024]{2,1,0:T(8,128)(2,1)}), bf16[32,8,1024]{2,1,0:T(8,128)(2,1)S(1)}, u32[]{:S(2)}, u32[]{:S(2)}) %all-to-all-start) | async-done | bytes 524320 | tf_op jit(solution)/shard_map/all_to_all | solution.py:184
  39.6 0.0 copy-start
  39.6 1.0 %copy-done = bf16[768,256]{1,0:T(8,128)(2,1)S(1)} copy-done((bf16[768,256]{1,0:T(8,128)(2,1)S(1)}, bf16[768,256]{1,0:T(8,128)(2,1)}, u32[]{:S(2)}) %copy-start) | copy-done | bytes 393240
  40.6 2.7 %shard_map.70 = (f32[8,128]{1,0:T(8,128)}, f32[8,128]{1,0:T(8,128)}) custom-call(bf16[256,1024]{1,0:T(8,128)(2,1)S(1)} %bitcast.4, bf16[768,256]{1,0:T(8,128)(2,1)S(1)} %copy-done), custom_call_target="tpu_custom_call" | custom-call | tf_op jit(solution)/shard_map/pallas_call | solution.py:169
Async XLA Ops:
  2.3 37.3 %all-to-all-start = ((bf16[32,8,1024]{2,1,0:T(8,128)(2,1)}), bf16[32,8,1024]{2,1,0:T(8,128)(2,1)S(1)}, u32[]{:S(2)}, u32[]{:S(2)}) async-start(bf16[32,8,1024]{2,1,0:T(8,128)(2,1)} %shard_map.68), calls=%async_computation | async-start | bytes 1048576 | tf_op jit(solution)/shard_map/all_to_all | solution.py:184
  39.6 1.0 %copy-start = (bf16[768,256]{1,0:T(8,128)(2,1)S(1)}, bf16[768,256]{1,0:T(8,128)(2,1)}, u32[]{:S(2)}) copy-start(bf16[768,256]{1,0:T(8,128)(2,1)} %shard_map.69.table_ref) | copy-start | bytes 1179652

commit v2 on v1

--- a/solution.py
+++ b/solution.py
@@ -149,7 +149,7 @@
 def pack(val, cond, val_energy, cond_energy, index):
     return pl.pallas_call(
         pack_kernel,
-        out_shape=jax.ShapeDtypeStruct((32, 8, 1024), jnp.bfloat16),
+        out_shape=pltpu.VMEM((32, 8, 1024), jnp.bfloat16),
         in_specs=[VMEM] * 5,
         out_specs=VMEM,
     )(val, cond, val_energy, cond_energy, index)
@@ -158,7 +158,7 @@
 def table(index):
     return pl.pallas_call(
         table_kernel,
-        out_shape=jax.ShapeDtypeStruct((NPTS, 256), jnp.bfloat16),
+        out_shape=pltpu.VMEM((NPTS, 256), jnp.bfloat16),
         in_specs=[VMEM],
         out_specs=VMEM,
         cost_estimate=pl.CostEstimate(flops=20_000_000, bytes_accessed=400_000, transcendentals=200_000),

time: 43.6 us -> 42.6 us (0.977)
  local copies, waits for them, and re-layouts: 1 us -> 0 us
  Pallas kernels: 7.49 us -> 6.74 us
  waiting for transfers between devices: 16.2 us -> 16.9 us
    unnamed x2 -> x0, local copies, waits for them, and re-layouts: 1 us -> none
    pallas_call x2, Pallas kernels: 4.8 us -> 4.05 us  [the longest x1 2.39 us: table(): pl.pallas_call(table_kernel, out_shape=pltpu.VMEM((NPTS, 256), jnp.bfloat...]
    all_to_all x1, waiting for transfers between devices: 16.2 us -> 16.9 us  [per_device(): lax.all_to_all(sent, ('val', 'cond'), 0, 0, tiled=True, axis_index_groups...]
  transfers between devices with their start and end apart: 1 -> 1, of which waited for: 1 -> 1; matrix products, arithmetic and copies ran while one was open for 0% -> 0% of each run, Pallas kernels for 7% -> 6%
where the time goes in v2:
time: 42.6 us; the launch traced here: 42.2 us
  starting transfers between devices  18 us (42%)
  waiting for transfers between devices  16.9 us (40%)
  Pallas kernels  6.74 us (16%)
  between operations  0.64 us (2%)
    all_to_all x1, starting transfers between devices, per_device(): lax.all_to_all(sent, ('val', 'cond'), 0, 0, tiled=True, axis_index_groups...  18 us
    all_to_all x1, waiting for transfers between devices, per_device(): lax.all_to_all(sent, ('val', 'cond'), 0, 0, tiled=True, axis_index_groups...  16.9 us
    pallas_call x1, Pallas kernels, chi(): pl.pallas_call(functools.partial(chi_kernel, factor), out_shape=[jax.Shap...  2.69 us
    pallas_call x1, Pallas kernels, table(): pl.pallas_call(table_kernel, out_shape=pltpu.VMEM((NPTS, 256), jnp.bfloat...  2.39 us
    pallas_call x1, Pallas kernels, pack(): pl.pallas_call(pack_kernel, out_shape=pltpu.VMEM((32, 8, 1024), jnp.bfloa...  1.66 us
  transfers between devices with their start and end apart: 1, of which 1 were waited for; matrix products, arithmetic and copies ran while one was open for 0% of the time, Pallas kernels for 6%

profile of v2, /device:TPU:1, one launch (start us, length us, event | category | flops | bytes accessed | tf_op | source)
XLA Modules:
  0.0 42.2 jit_solution(1680305310606511306)
XLA Ops:
  0.6 1.7 %shard_map.68 = bf16[32,8,1024]{2,1,0:T(8,128)(2,1)} custom-call(bf16[4,768]{1,0:T(4,128)(2,1)} %val_ref.1, bf16[8,768]{1,0:T(8,128)(2,1)} %cond_ref.1, bf16[1,4]{1,0:T(2,128)(2,1)} %bitcast.7, bf16[1,8]{1,0:T(2,128)(2,1)} %bitcast.8, s32[1,128]{1,0:T(1,128)} %bitcast.5), custom_call_target="tpu_custom_call" | custom-call | tf_op jit(solution)/shard_map/pallas_call | solution.py:150
  2.3 18.0 %all-to-all-start = ((bf16[32,8,1024]{2,1,0:T(8,128)(2,1)}), bf16[32,8,1024]{2,1,0:T(8,128)(2,1)S(1)}, u32[]{:S(2)}, u32[]{:S(2)}) async-start(bf16[32,8,1024]{2,1,0:T(8,128)(2,1)} %shard_map.68), calls=%async_computation | async-start | bytes 1048576 | tf_op jit(solution)/shard_map/all_to_all | solution.py:184
  20.3 2.4 %shard_map.69.table_ref = bf16[768,256]{1,0:T(8,128)(2,1)S(1)} custom-call(s32[1,128]{1,0:T(1,128)} %bitcast.6), custom_call_target="tpu_custom_call" | custom-call | flops 20000000 | bytes 400000 | tf_op jit(solution)/shard_map/pallas_call | solution.py:159
  22.6 16.9 %all-to-all-done = bf16[32,8,1024]{2,1,0:T(8,128)(2,1)S(1)} async-done(((bf16[32,8,1024]{2,1,0:T(8,128)(2,1)}), bf16[32,8,1024]{2,1,0:T(8,128)(2,1)S(1)}, u32[]{:S(2)}, u32[]{:S(2)}) %all-to-all-start) | async-done | bytes 524320 | tf_op jit(solution)/shard_map/all_to_all | solution.py:184
  39.6 2.7 %shard_map.70 = (f32[8,128]{1,0:T(8,128)}, f32[8,128]{1,0:T(8,128)}) custom-call(bf16[256,1024]{1,0:T(8,128)(2,1)S(1)} %bitcast.4, bf16[768,256]{1,0:T(8,128)(2,1)S(1)} %shard_map.69.table_ref), custom_call_target="tpu_custom_call" | custom-call | tf_op jit(solution)/shard_map/pallas_call | solution.py:169
Async XLA Ops:
  2.3 37.3 %all-to-all-start = ((bf16[32,8,1024]{2,1,0:T(8,128)(2,1)}), bf16[32,8,1024]{2,1,0:T(8,128)(2,1)S(1)}, u32[]{:S(2)}, u32[]{:S(2)}) async-start(bf16[32,8,1024]{2,1,0:T(8,128)(2,1)} %shard_map.68), calls=%async_computation | async-start | bytes 1048576 | tf_op jit(solution)/shard_map/all_to_all | solution.py:184

commit v3 on v2

v3 whole, which is shorter than its diff:
```python
import functools
import math

import jax
import jax.numpy as jnp
from jax import lax
from jax.experimental import pallas as pl
from jax.experimental.pallas import tpu as pltpu
from jax.sharding import PartitionSpec as P

NG = 96
SLAB_Y = 4
NPTS = 768
VMEM = pl.BlockSpec(memory_space=pltpu.VMEM)


def device_number(x, y, z, core):
    val = x * 4 + (y // 4) * 2 + core
    return val * 32 + z * 4 + y % 4


def groups():
    out = []
    for first_y in (2, 6):
        for x0 in range(4):
            for core in range(2):
                members = [
                    device_number((z + x0) % 4, (first_y + t) % 8, z, core)
                    for z in range(8)
                    for t in range(4)
                ]
                out.append(sorted(members, key=lambda d: d % 32))
    return out


def whole_part(value, divisor):
    return jnp.floor((value + 0.5) * (1.0 / divisor))


def components(index):
    flat = index.astype(jnp.float32)
    a = whole_part(flat, NG * NG)
    rest = flat - a * (NG * NG)
    b = whole_part(rest, NG)
    return a, b, rest - b * NG


def cos_sin(a, b, c, x, y, z):
    turns = a * x + b * y + c * z
    turns = turns - NG * whole_part(turns, NG)
    angles = turns * (2.0 * math.pi / NG)
    return jnp.cos(angles), jnp.sin(angles)


def grid_points(shape, dim):
    points = lax.broadcasted_iota(jnp.int32, shape, dim).astype(jnp.float32)
    z = whole_part(points, NG * SLAB_Y)
    rest = points - z * (NG * SLAB_Y)
    y = whole_part(rest, NG)
    return rest - y * NG, y, z


def dot(a, b, dims=(1, 0)):
    return lax.dot_general(
        a, b, (((dims[0],), (dims[1],)), ((), ())), preferred_element_type=jnp.float32
    )


def one_hot(condition):
    return jnp.where(condition, 1.0, 0.0).astype(jnp.bfloat16)


def iotas(rows, cols):
    return (
        lax.broadcasted_iota(jnp.int32, (rows, cols), 0),
        lax.broadcasted_iota(jnp.int32, (rows, cols), 1),
    )


def pack_kernel(val_ref, cond_ref, val_energy_ref, cond_energy_ref, index_ref, out_ref):
    cond = lax.axis_index("cond")
    share = 2 * (cond // 16) + lax.rem(cond, 2)
    row, lane = iotas(4, NPTS)
    val = jnp.sum(jnp.where(row == share, val_ref[...].astype(jnp.float32), 0.0), axis=0, keepdims=True)
    a, b, c = components(index_ref[...].reshape(1, 128))
    row, lane = iotas(1, 4)
    energy = jnp.sum(jnp.where(lane == share, val_energy_ref[...].astype(jnp.float32), 0.0), axis=1, keepdims=True)
    tail = jnp.concatenate(
        [cond_energy_ref[...].astype(jnp.float32), energy, jnp.zeros((1, 119), jnp.float32)], axis=1
    )
    rows = [val[:, 256 * q : 256 * q + 256] for q in range(3)]
    rows += [jnp.concatenate([a, b], axis=1), jnp.concatenate([c, tail], axis=1), jnp.zeros((3, 256), jnp.float32)]
    side = jnp.concatenate(rows, axis=0)
    block = jnp.concatenate([cond_ref[...].astype(jnp.float32), side], axis=1).astype(jnp.bfloat16)
    for k in range(out_ref.shape[0]):
        out_ref[k] = block


def chi_kernel(factor, got_ref, table_ref, mine_ref, other_ref, left_ref, weighted_ref):
    conduction = got_ref[:, 0:NPTS]
    side = got_ref[:, NPTS:]

    val = lax.axis_index("val")
    row, lane = iotas(16, 128)
    mine = lane == row + 16 * (val // 2)
    head = got_ref[0:16, NPTS:].astype(jnp.float32)

    def own(values):
        return jnp.sum(jnp.where(mine, values, 0.0), axis=1, keepdims=True)

    a, b, c = own(head[3:4, 0:128]), own(head[3:4, 128:256]), own(head[4:5, 0:128])
    window = jnp.concatenate(cos_sin(a, b, c, *grid_points((16, NPTS), 1)), axis=0).astype(jnp.bfloat16)
    window = window.astype(jnp.float32)

    v, r = iotas(32, 256)
    valence = jnp.concatenate([dot(one_hot(r == 8 * v + q), side) for q in range(3)], axis=1)
    energies = side[:, 128:256]
    picked = dot(one_hot(r == 8 * v + 4), energies)
    v, l = iotas(32, 128)
    val_energy = jnp.sum(jnp.where(l == 8, picked, 0.0), axis=1, keepdims=True)
    r, k = iotas(256, 256)
    spread = dot(energies, one_hot(r == 8 * (k // 8) + 4), (0, 0))
    l, k = iotas(128, 256)
    cond_energy = jnp.sum(jnp.where(l == k % 8, spread, 0.0), axis=0, keepdims=True)
    weights = factor / (cond_energy - val_energy)

    for j in range(32):
        left_ref[32 * j : 32 * j + 32, :] = (valence * window[j : j + 1, :]).astype(jnp.bfloat16)
    terms = dot(left_ref[...], conduction, (1, 1))
    for j in range(32):
        weighted_ref[32 * j : 32 * j + 32, :] = (terms[32 * j : 32 * j + 32, :] * weights).astype(jnp.bfloat16)
    back = dot(weighted_ref[...], conduction)
    totals = jnp.concatenate(
        [jnp.sum(back[32 * j : 32 * j + 32, :] * valence, axis=0, keepdims=True) for j in range(32)], axis=0
    )
    high = totals.astype(jnp.bfloat16)
    low = (totals - high.astype(jnp.float32)).astype(jnp.bfloat16)
    products = dot(high, table_ref[...]) + dot(low, table_ref[...])
    real = products[0:16, 0:128] + products[16:32, 128:256]
    imag = products[0:16, 128:256] - products[16:32, 0:128]
    both = jnp.concatenate([real, imag], axis=1)
    first = lax.rem(val, 2) == 0
    mine_ref[...] = jnp.where(first, both[0:8], both[8:16])
    other_ref[...] = jnp.where(first, both[8:16], both[0:8])


def table_kernel(index_ref, out_ref):
    a, b, c = components(index_ref[...].reshape(1, 128))
    cos, sin = cos_sin(a, b, c, *grid_points((NPTS, 1), 0))
    out_ref[:, 0:128] = cos.astype(jnp.bfloat16)
    out_ref[:, 128:256] = sin.astype(jnp.bfloat16)


def pack(val, cond, val_energy, cond_energy, index):
    return pl.pallas_call(
        pack_kernel,
        out_shape=pltpu.VMEM((32, 8, 1024), jnp.bfloat16),
        in_specs=[VMEM] * 5,
        out_specs=VMEM,
    )(val, cond, val_energy, cond_energy, index)


def table(index):
    return pl.pallas_call(
        table_kernel,
        out_shape=pltpu.VMEM((NPTS, 256), jnp.bfloat16),
        in_specs=[VMEM],
        out_specs=VMEM,
        cost_estimate=pl.CostEstimate(flops=20_000_000, bytes_accessed=400_000, transcendentals=200_000),
    )(index)


def chi(got, row_table, factor):
    return pl.pallas_call(
        functools.partial(chi_kernel, factor),
        out_shape=[jax.ShapeDtypeStruct((8, 256), jnp.float32)] * 2,
        in_specs=[VMEM] * 2,
        out_specs=[VMEM] * 2,
        scratch_shapes=[pltpu.VMEM((1024, NPTS), jnp.bfloat16), pltpu.VMEM((1024, 256), jnp.bfloat16)],
        compiler_params=pltpu.CompilerParams(vmem_limit_bytes=32 * 1024 * 1024),
    )(got, row_table)


def per_device(val_orbitals, cond_orbitals, val_energy, cond_energy, wave_index):
    factor = -4.0 / math.sqrt(4 * lax.axis_size("val") * 8 * lax.axis_size("cond"))
    sent = pack(
        val_orbitals, cond_orbitals, val_energy.reshape(1, 4), cond_energy.reshape(1, 8), wave_index.reshape(1, 128)
    )
    got = lax.all_to_all(sent, ("val", "cond"), 0, 0, tiled=True, axis_index_groups=groups())
    row_table = table(wave_index.reshape(1, 128))
    mine, other = chi(got.reshape(256, 1024), row_table, factor)
    theirs = lax.ppermute(other, "val", [(i, i ^ 1) for i in range(16)])
    return tuple(jnp.split(mine + theirs, 2, axis=1))


def solution(mesh):
    return jax.shard_map(
        per_device,
        mesh=mesh,
        in_specs=(P("val", None), P("cond", None), P("val"), P("cond"), P("cond")),
        out_specs=(P("val", "cond"), P("val", "cond")),
        check_vma=False,
    )
```

time: 42.6 us -> 45.8 us (1.075)
  starting transfers between devices: 18 us -> 21.7 us
  local copies, waits for them, and re-layouts: 0 us -> 0.6 us
  Pallas kernels: 6.74 us -> 6.16 us
  waiting for transfers between devices: 16.9 us -> 16.4 us
    ppermute x0 -> x1, starting transfers between devices: none -> 4.28 us  [per_device(): theirs = lax.ppermute(other, 'val', [(i, i ^ 1) for i in range(16)])]
    all_to_all x1, waiting for transfers between devices: 16.9 us -> 15.5 us  [per_device(): lax.all_to_all(sent, ('val', 'cond'), 0, 0, tiled=True, axis_index_groups...]
    ppermute x0 -> x1, waiting for transfers between devices: none -> 0.81 us  [per_device(): theirs = lax.ppermute(other, 'val', [(i, i ^ 1) for i in range(16)])]
    split x0 -> x1, local copies, waits for them, and re-layouts: none -> 0.6 us  [per_device(): return tuple(jnp.split(mine + theirs, 2, axis=1))]
    all_to_all x1, starting transfers between devices: 18 us -> 17.4 us  [per_device(): lax.all_to_all(sent, ('val', 'cond'), 0, 0, tiled=True, axis_index_groups...]
    pallas_call x1, Pallas kernels: 2.69 us -> 2.14 us  [chi(): pl.pallas_call(functools.partial(chi_kernel, factor), out_shape=[jax.Shap...]
  transfers between devices with their start and end apart: 1 -> 2, of which waited for: 1 -> 2; matrix products, arithmetic and copies ran while one was open for 0% -> 0% of each run, Pallas kernels for 6% -> 5%
where the time goes in v3:
time: 45.8 us; the launch traced here: 45.4 us
  starting transfers between devices  21.7 us (47%)
  waiting for transfers between devices  16.4 us (36%)
  Pallas kernels  6.16 us (13%)
  between operations  0.65 us (1%)
  local copies, waits for them, and re-layouts  0.6 us (1%)
    all_to_all x1, starting transfers between devices, per_device(): lax.all_to_all(sent, ('val', 'cond'), 0, 0, tiled=True, axis_index_groups...  17.4 us
    all_to_all x1, waiting for transfers between devices, per_device(): lax.all_to_all(sent, ('val', 'cond'), 0, 0, tiled=True, axis_index_groups...  15.5 us
    ppermute x1, starting transfers between devices, per_device(): theirs = lax.ppermute(other, 'val', [(i, i ^ 1) for i in range(16)])  4.28 us
    pallas_call x1, Pallas kernels, table(): pl.pallas_call(table_kernel, out_shape=pltpu.VMEM((NPTS, 256), jnp.bfloat...  2.39 us
    pallas_call x1, Pallas kernels, chi(): pl.pallas_call(functools.partial(chi_kernel, factor), out_shape=[jax.Shap...  2.14 us
    pallas_call x1, Pallas kernels, pack(): pl.pallas_call(pack_kernel, out_shape=pltpu.VMEM((32, 8, 1024), jnp.bfloa...  1.64 us
  transfers between devices with their start and end apart: 2, of which 2 were waited for; matrix products, arithmetic and copies ran while one was open for 0% of the time, Pallas kernels for 5%

profile of v3, /device:TPU:1, one launch (start us, length us, event | category | flops | bytes accessed | tf_op | source)
XLA Modules:
  0.0 45.4 jit_solution(8009377281403039550)
XLA Ops:
  0.6 1.6 %shard_map.68 = bf16[32,8,1024]{2,1,0:T(8,128)(2,1)} custom-call(bf16[4,768]{1,0:T(4,128)(2,1)} %val_ref.1, bf16[8,768]{1,0:T(8,128)(2,1)} %cond_ref.1, bf16[1,4]{1,0:T(2,128)(2,1)} %bitcast.7, bf16[1,8]{1,0:T(2,128)(2,1)} %bitcast.8, s32[1,128]{1,0:T(1,128)} %bitcast.5), custom_call_target="tpu_custom_call" | custom-call | tf_op jit(solution)/shard_map/pallas_call | solution.py:155
  2.3 17.4 %all-to-all-start = ((bf16[32,8,1024]{2,1,0:T(8,128)(2,1)}), bf16[32,8,1024]{2,1,0:T(8,128)(2,1)S(1)}, u32[]{:S(2)}, u32[]{:S(2)}) async-start(bf16[32,8,1024]{2,1,0:T(8,128)(2,1)} %shard_map.68), calls=%async_computation | async-start | bytes 1048576 | tf_op jit(solution)/shard_map/all_to_all | solution.py:189
  19.7 2.4 %shard_map.69.table_ref = bf16[768,256]{1,0:T(8,128)(2,1)S(1)} custom-call(s32[1,128]{1,0:T(1,128)} %bitcast.6), custom_call_target="tpu_custom_call" | custom-call | flops 20000000 | bytes 400000 | tf_op jit(solution)/shard_map/pallas_call | solution.py:164
  22.1 15.5 %all-to-all-done = bf16[32,8,1024]{2,1,0:T(8,128)(2,1)S(1)} async-done(((bf16[32,8,1024]{2,1,0:T(8,128)(2,1)}), bf16[32,8,1024]{2,1,0:T(8,128)(2,1)S(1)}, u32[]{:S(2)}, u32[]{:S(2)}) %all-to-all-start) | async-done | bytes 524320 | tf_op jit(solution)/shard_map/all_to_all | solution.py:189
  37.6 2.1 %shard_map.70 = (f32[8,256]{1,0:T(8,128)S(1)}, f32[8,256]{1,0:T(8,128)S(1)}) custom-call(bf16[256,1024]{1,0:T(8,128)(2,1)S(1)} %bitcast.4, bf16[768,256]{1,0:T(8,128)(2,1)S(1)} %shard_map.69.table_ref), custom_call_target="tpu_custom_call" | custom-call | tf_op jit(solution)/shard_map/pallas_call | solution.py:174
  39.7 4.3 %collective-permute-start = (f32[8,256]{1,0:T(8,128)S(1)}, f32[8,256]{1,0:T(8,128)S(1)}, u32[]{:S(2)}, u32[]{:S(2)}) collective-permute-start(f32[8,256]{1,0:T(8,128)S(1)} %get-tuple-element.5), channel_id=1, source_target_pairs={{0,32},{32,0},{64,96},{96,64},{128,160},{160,128},{192,224},{224,1... | collective-permute-start | bytes 24584 | tf_op jit(solution)/shard_map/ppermute | solution.py:192
  44.0 0.8 %collective-permute-done = f32[8,256]{1,0:T(8,128)S(1)} collective-permute-done((f32[8,256]{1,0:T(8,128)S(1)}, f32[8,256]{1,0:T(8,128)S(1)}, u32[]{:S(2)}, u32[]{:S(2)}) %collective-permute-start) | collective-permute-done | bytes 8224 | tf_op jit(solution)/shard_map/ppermute | solution.py:192
  44.8 0.6 %fusion = (f32[8,128]{1,0:T(8,128)}, f32[8,128]{1,0:T(8,128)}) fusion(f32[8,256]{1,0:T(8,128)S(1)} %add.3), kind=kLoop, calls=%fused_computation | loop fusion | bytes 16384 | tf_op jit(solution)/shard_map/split | solution.py:193
  (1 shorter events, 0.0 us)
Async XLA Ops:
  2.3 35.3 %all-to-all-start = ((bf16[32,8,1024]{2,1,0:T(8,128)(2,1)}), bf16[32,8,1024]{2,1,0:T(8,128)(2,1)S(1)}, u32[]{:S(2)}, u32[]{:S(2)}) async-start(bf16[32,8,1024]{2,1,0:T(8,128)(2,1)} %shard_map.68), calls=%async_computation | async-start | bytes 1048576 | tf_op jit(solution)/shard_map/all_to_all | solution.py:189
  39.7 5.1 %collective-permute-start = (f32[8,256]{1,0:T(8,128)S(1)}, f32[8,256]{1,0:T(8,128)S(1)}, u32[]{:S(2)}, u32[]{:S(2)}) collective-permute-start(f32[8,256]{1,0:T(8,128)S(1)} %get-tuple-element.5), channel_id=1, source_target_pairs={{0,32},{32,0},{64,96},{96,64},{128,160},{160,128},{192,224},{224,1... | collective-permute-start | bytes 24584 | tf_op jit(solution)/shard_map/ppermute | solution.py:192

commit v4 on v2

--- a/solution.py
+++ b/solution.py
@@ -11,6 +11,7 @@
 NG = 96
 SLAB_Y = 4
 NPTS = 768
+STEP = 4
 VMEM = pl.BlockSpec(memory_space=pltpu.VMEM)
 
 
@@ -95,7 +96,21 @@
     )
 
 
-def chi_kernel(factor, got_ref, table_ref, real_ref, imag_ref, left_ref, weighted_ref):
+def phase_table(index):
+    a, b, c = components(index)
+    x = lax.broadcasted_iota(jnp.int32, (NG, 1), 0).astype(jnp.float32)
+    cos_x, sin_x = cos_sin(a, b, c, x, 0.0, 0.0)
+    line = lax.broadcasted_iota(jnp.int32, (NPTS // NG, 1), 0).astype(jnp.float32)
+    z = whole_part(line, SLAB_Y)
+    cos_l, sin_l = cos_sin(a, b, c, 0.0, line - z * SLAB_Y, z)
+    blocks = []
+    for k in range(NPTS // NG):
+        ck, sk = cos_l[k : k + 1], sin_l[k : k + 1]
+        blocks.append(jnp.concatenate([cos_x * ck - sin_x * sk, sin_x * ck + cos_x * sk], axis=1).astype(jnp.bfloat16))
+    return jnp.concatenate(blocks, axis=0)
+
+
+def chi_kernel(factor, got_ref, index_ref, real_ref, imag_ref):
     conduction = got_ref[:, 0:NPTS]
     side = got_ref[:, NPTS:]
 
@@ -108,11 +123,11 @@
 
     a, b, c = own(head[6:7, 0:128]), own(head[6:7, 128:256]), own(head[7:8, 0:128])
     window = jnp.concatenate(cos_sin(a, b, c, *grid_points((8, NPTS), 1)), axis=0).astype(jnp.bfloat16)
-    window = window.astype(jnp.float32)
 
     v, r = iotas(64, 256)
     first = 8 * (v // 2) + 3 * (v % 2)
     valence = jnp.concatenate([dot(one_hot(r == first + q), side) for q in range(3)], axis=1)
+    narrow = valence.astype(jnp.bfloat16)
     energies = side[:, 128:256]
     picked = dot(one_hot(r == 8 * (v // 2) + 7), energies)
     v, l = iotas(64, 128)
@@ -123,27 +138,21 @@
     cond_energy = jnp.sum(jnp.where(l == k % 8, spread, 0.0), axis=0, keepdims=True)
     weights = factor / (cond_energy - val_energy)
 
-    for j in range(16):
-        left_ref[64 * j : 64 * j + 64, :] = (valence * window[j : j + 1, :]).astype(jnp.bfloat16)
-    terms = dot(left_ref[...], conduction, (1, 1))
-    for j in range(16):
-        weighted_ref[64 * j : 64 * j + 64, :] = (terms[64 * j : 64 * j + 64, :] * weights).astype(jnp.bfloat16)
-    back = dot(weighted_ref[...], conduction)
-    totals = jnp.concatenate(
-        [jnp.sum(back[64 * j : 64 * j + 64, :] * valence, axis=0, keepdims=True) for j in range(16)], axis=0
-    )
+    totals = []
+    for start in range(0, 16, STEP):
+        left = jnp.concatenate([narrow * window[j : j + 1, :] for j in range(start, start + STEP)], axis=0)
+        terms = dot(left, conduction, (1, 1))
+        weighted = [(terms[64 * i : 64 * i + 64] * weights).astype(jnp.bfloat16) for i in range(STEP)]
+        back = dot(jnp.concatenate(weighted, axis=0), conduction)
+        totals += [jnp.sum(back[64 * i : 64 * i + 64] * valence, axis=0, keepdims=True) for i in range(STEP)]
+    totals = jnp.concatenate(totals, axis=0)
+
+    table = phase_table(index_ref[...])
     high = totals.astype(jnp.bfloat16)
     low = (totals - high.astype(jnp.float32)).astype(jnp.bfloat16)
-    products = dot(high, table_ref[...]) + dot(low, table_ref[...])
+    products = dot(high, table) + dot(low, table)
     real_ref[...] = products[0:8, 0:128] + products[8:16, 128:256]
     imag_ref[...] = products[0:8, 128:256] - products[8:16, 0:128]
-
-
-def table_kernel(index_ref, out_ref):
-    a, b, c = components(index_ref[...].reshape(1, 128))
-    cos, sin = cos_sin(a, b, c, *grid_points((NPTS, 1), 0))
-    out_ref[:, 0:128] = cos.astype(jnp.bfloat16)
-    out_ref[:, 128:256] = sin.astype(jnp.bfloat16)
 
 
 def pack(val, cond, val_energy, cond_energy, index):
@@ -155,25 +164,14 @@
     )(val, cond, val_energy, cond_energy, index)
 
 
-def table(index):
-    return pl.pallas_call(
-        table_kernel,
-        out_shape=pltpu.VMEM((NPTS, 256), jnp.bfloat16),
-        in_specs=[VMEM],
-        out_specs=VMEM,
-        cost_estimate=pl.CostEstimate(flops=20_000_000, bytes_accessed=400_000, transcendentals=200_000),
-    )(index)
-
-
-def chi(got, row_table, factor):
+def chi(got, index, factor):
     return pl.pallas_call(
         functools.partial(chi_kernel, factor),
         out_shape=[jax.ShapeDtypeStruct((8, 128), jnp.float32)] * 2,
         in_specs=[VMEM] * 2,
         out_specs=[VMEM] * 2,
-        scratch_shapes=[pltpu.VMEM((1024, NPTS), jnp.bfloat16), pltpu.VMEM((1024, 256), jnp.bfloat16)],
         compiler_params=pltpu.CompilerParams(vmem_limit_bytes=32 * 1024 * 1024),
-    )(got, row_table)
+    )(got, index)
 
 
 def per_device(val_orbitals, cond_orbitals, val_energy, cond_energy, wave_index):
@@ -182,8 +180,7 @@
         val_orbitals, cond_orbitals, val_energy.reshape(1, 4), cond_energy.reshape(1, 8), wave_index.reshape(1, 128)
     )
     got = lax.all_to_all(sent, ("val", "cond"), 0, 0, tiled=True, axis_index_groups=groups())
-    row_table = table(wave_index.reshape(1, 128))
-    return tuple(chi(got.reshape(256, 1024), row_table, factor))
+    return tuple(chi(got.reshape(256, 1024), wave_index.reshape(1, 128), factor))
 
 
 def solution(mesh):

time: 42.6 us -> 41.9 us (0.984)
  blocking collectives: 0 us -> 37.1 us
  starting transfers between devices: 18 us -> 0 us
  waiting for transfers between devices: 16.9 us -> 0 us
  Pallas kernels: 6.74 us -> 3.37 us
  local copies, waits for them, and re-layouts: 0 us -> 0.66 us
    all_to_all x0 -> x1, blocking collectives: none -> 37.1 us  [per_device(): lax.all_to_all(sent, ('val', 'cond'), 0, 0, tiled=True, axis_index_groups...]
    all_to_all x1 -> x0, starting transfers between devices: 18 us -> none  [per_device(): lax.all_to_all(sent, ('val', 'cond'), 0, 0, tiled=True, axis_index_groups...]
    all_to_all x1 -> x0, waiting for transfers between devices: 16.9 us -> none  [per_device(): lax.all_to_all(sent, ('val', 'cond'), 0, 0, tiled=True, axis_index_groups...]
    pallas_call x1 -> x0, Pallas kernels: 2.39 us -> none  [table(): pl.pallas_call(table_kernel, out_shape=pltpu.VMEM((NPTS, 256), jnp.bfloat...]
    pallas_call x1, Pallas kernels: 1.66 us -> 0.88 us  [pack(): pl.pallas_call(pack_kernel, out_shape=pltpu.VMEM((32, 8, 1024), jnp.bfloa...]
    unnamed x0 -> x2, local copies, waits for them, and re-layouts: none -> 0.66 us
  transfers between devices with their start and end apart: 1 -> 0, of which waited for: 1 -> 0; matrix products, arithmetic and copies ran while one was open for 0% -> 0% of each run, Pallas kernels for 6% -> 0%
where the time goes in v4:
time: 41.9 us; the launch traced here: 41.7 us
  blocking collectives  37.1 us (89%)
  Pallas kernels  3.37 us (8%)
  local copies, waits for them, and re-layouts  0.66 us (2%)
  between operations  0.64 us (2%)
    all_to_all x1, blocking collectives, per_device(): lax.all_to_all(sent, ('val', 'cond'), 0, 0, tiled=True, axis_index_groups...  37.1 us
    pallas_call x1, Pallas kernels, chi(): pl.pallas_call(functools.partial(chi_kernel, factor), out_shape=[jax.Shap...  2.49 us
    pallas_call x1, Pallas kernels, pack(): pl.pallas_call(pack_kernel, out_shape=pltpu.VMEM((32, 8, 1024), jnp.bfloa...  0.88 us

profile of v4, /device:TPU:1, one launch (start us, length us, event | category | flops | bytes accessed | tf_op | source)
XLA Modules:
  0.0 41.7 jit_solution(6213229137448912688)
XLA Ops:
  0.6 0.9 %shard_map.68 = bf16[32,8,1024]{2,1,0:T(8,128)(2,1)S(1)} custom-call(bf16[4,768]{1,0:T(4,128)(2,1)} %val_ref.1, bf16[8,768]{1,0:T(8,128)(2,1)} %cond_ref.1, bf16[1,4]{1,0:T(2,128)(2,1)} %bitcast.7, bf16[1,8]{1,0:T(2,128)(2,1)} %bitcast.8, s32[1,128]{1,0:T(1,128)} %bitcast.5), custom_call_target="tpu_custom_call" | custom-call | tf_op jit(solution)/shard_map/pallas_call | solution.py:159
  1.5 37.1 %all_to_all.5 = bf16[32,8,1024]{2,1,0:T(8,128)(2,1)S(1)} all-to-all(bf16[32,8,1024]{2,1,0:T(8,128)(2,1)S(1)} %shard_map.68), channel_id=1, replica_groups={{64,65,2,3,196,197,134,135,328,329,266,267,460,461,398,399,112,113,50,5..., dimensions={0} | all-to-all | bytes 1048576 | tf_op jit(solution)/shard_map/all_to_all | solution.py:182
  38.6 0.0 copy-start
  38.6 0.7 %copy-done = s32[128]{0:T(128)S(1)} copy-done((s32[128]{0:T(128)S(1)}, s32[128]{0:T(128)}, u32[]{:S(2)}) %copy-start) | copy-done | bytes 536
  39.2 2.5 %shard_map.69 = (f32[8,128]{1,0:T(8,128)}, f32[8,128]{1,0:T(8,128)}) custom-call(bf16[256,1024]{1,0:T(8,128)(2,1)S(1)} %bitcast.4, s32[1,128]{1,0:T(1,128)S(1)} %bitcast.6), custom_call_target="tpu_custom_call" | custom-call | tf_op jit(solution)/shard_map/pallas_call | solution.py:168
Async XLA Ops:
  38.6 0.7 %copy-start = (s32[128]{0:T(128)S(1)}, s32[128]{0:T(128)}, u32[]{:S(2)}) copy-start(s32[128]{0:T(128)} %param.9) | copy-start | bytes 1540

commit v5 on v4

--- a/solution.py
+++ b/solution.py
@@ -11,7 +11,7 @@
 NG = 96
 SLAB_Y = 4
 NPTS = 768
-STEP = 4
+STEP = 8
 VMEM = pl.BlockSpec(memory_space=pltpu.VMEM)
 
 
@@ -26,7 +26,7 @@
         for x0 in range(4):
             for core0 in range(2):
                 members = [
-                    device_number((z + x0) % 4, (first_y + t) % 8, z, (core0 + z // 4) % 2)
+                    device_number((z + x0) % 4, (first_y + t) % 8, z, (core0 + t) % 2)
                     for z in range(8)
                     for t in range(4)
                 ]
@@ -61,13 +61,14 @@
     return rest - y * NG, y, z
 
 
-def pack_kernel(val_ref, cond_ref, val_energy_ref, cond_energy_ref, index_ref, out_ref):
-    odd = lax.rem(lax.axis_index("cond"), 2) == 1
+def pack_kernel(val_ref, cond_ref, val_energy_ref, cond_energy_ref, index_ref, out_ref, own_ref):
+    upper = lax.axis_index("cond") >= 16
     val = val_ref[...].astype(jnp.float32)
-    val = jnp.where(odd, val[2:4], val[0:2])
-    a, b, c = components(index_ref[...].reshape(1, 128))
+    val = jnp.where(upper, val[2:4], val[0:2])
+    a, b, c = components(index_ref[...])
+    own_ref[...] = jnp.concatenate([a, b, c, jnp.zeros((5, 128), jnp.float32)], axis=0)
     energy = val_energy_ref[...].astype(jnp.float32)
-    energy = jnp.where(odd, energy[:, 2:4], energy[:, 0:2])
+    energy = jnp.where(upper, energy[:, 2:4], energy[:, 0:2])
     tail = jnp.concatenate(
         [cond_energy_ref[...].astype(jnp.float32), energy, jnp.zeros((1, 118), jnp.float32)], axis=1
     )
@@ -96,8 +97,7 @@
     )
 
 
-def phase_table(index):
-    a, b, c = components(index)
+def phase_table(a, b, c):
     x = lax.broadcasted_iota(jnp.int32, (NG, 1), 0).astype(jnp.float32)
     cos_x, sin_x = cos_sin(a, b, c, x, 0.0, 0.0)
     line = lax.broadcasted_iota(jnp.int32, (NPTS // NG, 1), 0).astype(jnp.float32)
@@ -110,7 +110,7 @@
     return jnp.concatenate(blocks, axis=0)
 
 
-def chi_kernel(factor, got_ref, index_ref, real_ref, imag_ref):
+def chi_kernel(factor, got_ref, own_ref, real_ref, imag_ref):
     conduction = got_ref[:, 0:NPTS]
     side = got_ref[:, NPTS:]
 
@@ -138,16 +138,22 @@
     cond_energy = jnp.sum(jnp.where(l == k % 8, spread, 0.0), axis=0, keepdims=True)
     weights = factor / (cond_energy - val_energy)
 
+    lefts = [
+        jnp.concatenate([narrow * window[j : j + 1, :] for j in range(start, start + STEP)], axis=0)
+        for start in range(0, 16, STEP)
+    ]
     totals = []
-    for start in range(0, 16, STEP):
-        left = jnp.concatenate([narrow * window[j : j + 1, :] for j in range(start, start + STEP)], axis=0)
-        terms = dot(left, conduction, (1, 1))
+    ahead = dot(lefts[0], conduction, (1, 1))
+    for following in [*lefts[1:], None]:
+        terms = ahead
+        if following is not None:
+            ahead = dot(following, conduction, (1, 1))
         weighted = [(terms[64 * i : 64 * i + 64] * weights).astype(jnp.bfloat16) for i in range(STEP)]
         back = dot(jnp.concatenate(weighted, axis=0), conduction)
         totals += [jnp.sum(back[64 * i : 64 * i + 64] * valence, axis=0, keepdims=True) for i in range(STEP)]
     totals = jnp.concatenate(totals, axis=0)
 
-    table = phase_table(index_ref[...])
+    table = phase_table(own_ref[0:1], own_ref[1:2], own_ref[2:3])
     high = totals.astype(jnp.bfloat16)
     low = (totals - high.astype(jnp.float32)).astype(jnp.bfloat16)
     products = dot(high, table) + dot(low, table)
@@ -158,29 +164,29 @@
 def pack(val, cond, val_energy, cond_energy, index):
     return pl.pallas_call(
         pack_kernel,
-        out_shape=pltpu.VMEM((32, 8, 1024), jnp.bfloat16),
+        out_shape=[pltpu.VMEM((32, 8, 1024), jnp.bfloat16), pltpu.VMEM((8, 128), jnp.float32)],
         in_specs=[VMEM] * 5,
-        out_specs=VMEM,
+        out_specs=[VMEM] * 2,
     )(val, cond, val_energy, cond_energy, index)
 
 
-def chi(got, index, factor):
+def chi(got, own, factor):
     return pl.pallas_call(
         functools.partial(chi_kernel, factor),
         out_shape=[jax.ShapeDtypeStruct((8, 128), jnp.float32)] * 2,
         in_specs=[VMEM] * 2,
         out_specs=[VMEM] * 2,
         compiler_params=pltpu.CompilerParams(vmem_limit_bytes=32 * 1024 * 1024),
-    )(got, index)
+    )(got, own)
 
 
 def per_device(val_orbitals, cond_orbitals, val_energy, cond_energy, wave_index):
     factor = -4.0 / math.sqrt(4 * lax.axis_size("val") * 8 * lax.axis_size("cond"))
-    sent = pack(
+    sent, own = pack(
         val_orbitals, cond_orbitals, val_energy.reshape(1, 4), cond_energy.reshape(1, 8), wave_index.reshape(1, 128)
     )
     got = lax.all_to_all(sent, ("val", "cond"), 0, 0, tiled=True, axis_index_groups=groups())
-    return tuple(chi(got.reshape(256, 1024), wave_index.reshape(1, 128), factor))
+    return tuple(chi(got.reshape(256, 1024), own, factor))
 
 
 def solution(mesh):

time: 41.9 us -> 40.6 us (0.969)
  local copies, waits for them, and re-layouts: 0.66 us -> 0 us
    unnamed x2 -> x0, local copies, waits for them, and re-layouts: 0.66 us -> none
where the time goes in v5:
time: 40.6 us; the launch traced here: 40.4 us
  blocking collectives  36.7 us (90%)
  Pallas kernels  3.06 us (8%)
  between operations  0.64 us (2%)
    all_to_all x1, blocking collectives, per_device(): lax.all_to_all(sent, ('val', 'cond'), 0, 0, tiled=True, axis_index_groups...  36.7 us
    pallas_call x1, Pallas kernels, chi(): pl.pallas_call(functools.partial(chi_kernel, factor), out_shape=[jax.Shap...  2.18 us
    pallas_call x1, Pallas kernels, pack(): pl.pallas_call(pack_kernel, out_shape=[pltpu.VMEM((32, 8, 1024), jnp.bflo...  0.88 us

profile of v5, /device:TPU:1, one launch (start us, length us, event | category | flops | bytes accessed | tf_op | source)
XLA Modules:
  0.0 40.4 jit_solution(4401732476684324899)
XLA Ops:
  0.6 0.9 %shard_map.68 = (bf16[32,8,1024]{2,1,0:T(8,128)(2,1)S(1)}, f32[8,128]{1,0:T(8,128)S(1)}) custom-call(bf16[4,768]{1,0:T(4,128)(2,1)} %val_ref.1, bf16[8,768]{1,0:T(8,128)(2,1)} %cond_ref.1, bf16[1,4]{1,0:T(2,128)(2,1)} %bitcast.5, bf16[1,8]{1,0:T(2,128)(2,1)} %bitcast.6, s32[1,128]{1,0:T(1,128)} %bitcast.7), custom_call_target="tpu_custom_call" | custom-call | tf_op jit(solution)/shard_map/pallas_call | solution.py:165
  1.5 36.7 %all_to_all.5 = bf16[32,8,1024]{2,1,0:T(8,128)(2,1)S(1)} all-to-all(bf16[32,8,1024]{2,1,0:T(8,128)(2,1)S(1)} %get-tuple-element.4), channel_id=1, replica_groups={{64,97,2,35,196,229,134,167,328,361,266,299,460,493,398,431,80,113,18,5..., dimensions={0} | all-to-all | bytes 1048576 | tf_op jit(solution)/shard_map/all_to_all | solution.py:188
  38.2 2.2 %shard_map.69 = (f32[8,128]{1,0:T(8,128)}, f32[8,128]{1,0:T(8,128)}) custom-call(bf16[256,1024]{1,0:T(8,128)(2,1)S(1)} %bitcast.4, f32[8,128]{1,0:T(8,128)S(1)} %get-tuple-element.5.own_ref), custom_call_target="tpu_custom_call" | custom-call | tf_op jit(solution)/shard_map/pallas_call | solution.py:174

commit v6 on v5

--- a/solution.py
+++ b/solution.py
@@ -26,11 +26,11 @@
         for x0 in range(4):
             for core0 in range(2):
                 members = [
-                    device_number((z + x0) % 4, (first_y + t) % 8, z, (core0 + t) % 2)
+                    device_number((z + t % 2 + x0) % 4, (first_y + t) % 8, z, (core0 + z // 4) % 2)
                     for z in range(8)
                     for t in range(4)
                 ]
-                out.append(sorted(members, key=lambda d: d % 32))
+                out.append(members)
     return out
 
 
@@ -62,13 +62,13 @@
 
 
 def pack_kernel(val_ref, cond_ref, val_energy_ref, cond_energy_ref, index_ref, out_ref, own_ref):
-    upper = lax.axis_index("cond") >= 16
+    odd = lax.rem(lax.axis_index("cond"), 2) == 1
     val = val_ref[...].astype(jnp.float32)
-    val = jnp.where(upper, val[2:4], val[0:2])
+    val = jnp.where(odd, val[2:4], val[0:2])
     a, b, c = components(index_ref[...])
     own_ref[...] = jnp.concatenate([a, b, c, jnp.zeros((5, 128), jnp.float32)], axis=0)
     energy = val_energy_ref[...].astype(jnp.float32)
-    energy = jnp.where(upper, energy[:, 2:4], energy[:, 0:2])
+    energy = jnp.where(odd, energy[:, 2:4], energy[:, 0:2])
     tail = jnp.concatenate(
         [cond_energy_ref[...].astype(jnp.float32), energy, jnp.zeros((1, 118), jnp.float32)], axis=1
     )
@@ -116,7 +116,7 @@
 
     row, lane = iotas(8, 128)
     mine = lane == row + 8 * lax.axis_index("val")
-    head = got_ref[0:16, NPTS:].astype(jnp.float32)
+    head = got_ref[16:32, NPTS:].astype(jnp.float32)
 
     def own(values):
         return jnp.sum(jnp.where(mine, values, 0.0), axis=1, keepdims=True)

time: 40.6 us -> 39.9 us (0.983)
  blocking collectives: 36.7 us -> 36 us
    all_to_all x1, blocking collectives: 36.7 us -> 36 us  [per_device(): lax.all_to_all(sent, ('val', 'cond'), 0, 0, tiled=True, axis_index_groups...]
where the time goes in v6:
time: 39.9 us; the launch traced here: 39.7 us
  blocking collectives  36 us (90%)
  Pallas kernels  3.06 us (8%)
  between operations  0.64 us (2%)
    all_to_all x1, blocking collectives, per_device(): lax.all_to_all(sent, ('val', 'cond'), 0, 0, tiled=True, axis_index_groups...  36 us
    pallas_call x1, Pallas kernels, chi(): pl.pallas_call(functools.partial(chi_kernel, factor), out_shape=[jax.Shap...  2.18 us
    pallas_call x1, Pallas kernels, pack(): pl.pallas_call(pack_kernel, out_shape=[pltpu.VMEM((32, 8, 1024), jnp.bflo...  0.88 us

profile of v6, /device:TPU:1, one launch (start us, length us, event | category | flops | bytes accessed | tf_op | source)
XLA Modules:
  0.0 39.7 jit_solution(2291936187449754963)
XLA Ops:
  0.6 0.9 %shard_map.68 = (bf16[32,8,1024]{2,1,0:T(8,128)(2,1)S(1)}, f32[8,128]{1,0:T(8,128)S(1)}) custom-call(bf16[4,768]{1,0:T(4,128)(2,1)} %val_ref.1, bf16[8,768]{1,0:T(8,128)(2,1)} %cond_ref.1, bf16[1,4]{1,0:T(2,128)(2,1)} %bitcast.5, bf16[1,8]{1,0:T(2,128)(2,1)} %bitcast.6, s32[1,128]{1,0:T(1,128)} %bitcast.7), custom_call_target="tpu_custom_call" | custom-call | tf_op jit(solution)/shard_map/pallas_call | solution.py:165
  1.5 36.0 %all_to_all.5 = bf16[32,8,1024]{2,1,0:T(8,128)(2,1)S(1)} all-to-all(bf16[32,8,1024]{2,1,0:T(8,128)(2,1)S(1)} %get-tuple-element.4), channel_id=1, replica_groups={{2,131,64,193,134,263,196,325,266,395,328,457,398,15,460,77,50,179,112,..., dimensions={0} | all-to-all | bytes 1048576 | tf_op jit(solution)/shard_map/all_to_all | solution.py:188
  37.5 2.2 %shard_map.69 = (f32[8,128]{1,0:T(8,128)}, f32[8,128]{1,0:T(8,128)}) custom-call(bf16[256,1024]{1,0:T(8,128)(2,1)S(1)} %bitcast.4, f32[8,128]{1,0:T(8,128)S(1)} %get-tuple-element.5.own_ref), custom_call_target="tpu_custom_call" | custom-call | tf_op jit(solution)/shard_map/pallas_call | solution.py:174

commit v7 on v6

--- a/solution.py
+++ b/solution.py
@@ -27,7 +27,7 @@
             for core0 in range(2):
                 members = [
                     device_number((z + t % 2 + x0) % 4, (first_y + t) % 8, z, (core0 + z // 4) % 2)
-                    for z in range(8)
+                    for z in reversed(range(8))
                     for t in range(4)
                 ]
                 out.append(members)
@@ -116,7 +116,7 @@
 
     row, lane = iotas(8, 128)
     mine = lane == row + 8 * lax.axis_index("val")
-    head = got_ref[16:32, NPTS:].astype(jnp.float32)
+    head = got_ref[240:256, NPTS:].astype(jnp.float32)
 
     def own(values):
         return jnp.sum(jnp.where(mine, values, 0.0), axis=1, keepdims=True)

time: 39.9 us -> 38 us (0.952)
  the two profiles are of different devices: /device:TPU:1 before, /device:TPU:17 now
where the time goes in v7:
time: 38 us; the launch traced here: 37.8 us
  blocking collectives  34.1 us (90%)
  Pallas kernels  3.07 us (8%)
  between operations  0.64 us (2%)
    all_to_all x1, blocking collectives, per_device(): lax.all_to_all(sent, ('val', 'cond'), 0, 0, tiled=True, axis_index_groups...  34.1 us
    pallas_call x1, Pallas kernels, chi(): pl.pallas_call(functools.partial(chi_kernel, factor), out_shape=[jax.Shap...  2.19 us
    pallas_call x1, Pallas kernels, pack(): pl.pallas_call(pack_kernel, out_shape=[pltpu.VMEM((32, 8, 1024), jnp.bflo...  0.88 us

profile of v7, /device:TPU:17, one launch (start us, length us, event | category | flops | bytes accessed | tf_op | source)
XLA Modules:
  0.0 37.8 jit_solution(10556763514084087343)
XLA Ops:
  0.6 0.9 %shard_map.68 = (bf16[32,8,1024]{2,1,0:T(8,128)(2,1)S(1)}, f32[8,128]{1,0:T(8,128)S(1)}) custom-call(bf16[4,768]{1,0:T(4,128)(2,1)} %val_ref.1, bf16[8,768]{1,0:T(8,128)(2,1)} %cond_ref.1, bf16[1,4]{1,0:T(2,128)(2,1)} %bitcast.5, bf16[1,8]{1,0:T(2,128)(2,1)} %bitcast.6, s32[1,128]{1,0:T(1,128)} %bitcast.7), custom_call_target="tpu_custom_call" | custom-call | tf_op jit(solution)/shard_map/pallas_call | solution.py:165
  1.5 34.1 %all_to_all.5 = bf16[32,8,1024]{2,1,0:T(8,128)(2,1)S(1)} all-to-all(bf16[32,8,1024]{2,1,0:T(8,128)(2,1)S(1)} %get-tuple-element.4), channel_id=1, replica_groups={{446,63,508,125,314,443,376,505,182,311,244,373,50,179,112,241,398,15,4..., dimensions={0} | all-to-all | bytes 1048576 | tf_op jit(solution)/shard_map/all_to_all | solution.py:188
  35.6 2.2 %shard_map.69 = (f32[8,128]{1,0:T(8,128)}, f32[8,128]{1,0:T(8,128)}) custom-call(bf16[256,1024]{1,0:T(8,128)(2,1)S(1)} %bitcast.4, f32[8,128]{1,0:T(8,128)S(1)} %get-tuple-element.5.own_ref), custom_call_target="tpu_custom_call" | custom-call | tf_op jit(solution)/shard_map/pallas_call | solution.py:174

commit v8 on v7

--- a/solution.py
+++ b/solution.py
@@ -22,13 +22,13 @@
 
 def groups():
     out = []
-    for first_y in (2, 6):
+    for first_y, order in ((2, (2, 3, 0, 1)), (6, (0, 1, 2, 3))):
         for x0 in range(4):
             for core0 in range(2):
                 members = [
                     device_number((z + t % 2 + x0) % 4, (first_y + t) % 8, z, (core0 + z // 4) % 2)
                     for z in reversed(range(8))
-                    for t in range(4)
+                    for t in order
                 ]
                 out.append(members)
     return out
@@ -116,7 +116,10 @@
 
     row, lane = iotas(8, 128)
     mine = lane == row + 8 * lax.axis_index("val")
-    head = got_ref[240:256, NPTS:].astype(jnp.float32)
+    y_high, y_low = lax.rem(lax.axis_index("val") // 2, 2), lax.rem(lax.axis_index("cond"), 4)
+    middle = (y_high == 0) == (y_low >= 2)
+    last = got_ref[224:256, NPTS:].astype(jnp.float32)
+    head = jnp.where(middle, last[0:16], last[16:32])
 
     def own(values):
         return jnp.sum(jnp.where(mine, values, 0.0), axis=1, keepdims=True)

time: 38 us -> 37.4 us (0.984)
  the two profiles are of different devices: /device:TPU:17 before, /device:TPU:1 now
where the time goes in v8:
time: 37.4 us; the launch traced here: 37.2 us
  blocking collectives  33.5 us (90%)
  Pallas kernels  3.07 us (8%)
  between operations  0.64 us (2%)
    all_to_all x1, blocking collectives, per_device(): lax.all_to_all(sent, ('val', 'cond'), 0, 0, tiled=True, axis_index_groups...  33.5 us
    pallas_call x1, Pallas kernels, chi(): pl.pallas_call(functools.partial(chi_kernel, factor), out_shape=[jax.Shap...  2.19 us
    pallas_call x1, Pallas kernels, pack(): pl.pallas_call(pack_kernel, out_shape=[pltpu.VMEM((32, 8, 1024), jnp.bflo...  0.88 us

profile of v8, /device:TPU:1, one launch (start us, length us, event | category | flops | bytes accessed | tf_op | source)
XLA Modules:
  0.0 37.2 jit_solution(5052292369906107488)
XLA Ops:
  0.6 0.9 %shard_map.68 = (bf16[32,8,1024]{2,1,0:T(8,128)(2,1)S(1)}, f32[8,128]{1,0:T(8,128)S(1)}) custom-call(bf16[4,768]{1,0:T(4,128)(2,1)} %val_ref.1, bf16[8,768]{1,0:T(8,128)(2,1)} %cond_ref.1, bf16[1,4]{1,0:T(2,128)(2,1)} %bitcast.5, bf16[1,8]{1,0:T(2,128)(2,1)} %bitcast.6, s32[1,128]{1,0:T(1,128)} %bitcast.7), custom_call_target="tpu_custom_call" | custom-call | tf_op jit(solution)/shard_map/pallas_call | solution.py:168
  1.5 33.5 %all_to_all.5 = bf16[32,8,1024]{2,1,0:T(8,128)(2,1)S(1)} all-to-all(bf16[32,8,1024]{2,1,0:T(8,128)(2,1)S(1)} %get-tuple-element.4), channel_id=1, replica_groups={{508,125,446,63,376,505,314,443,244,373,182,311,112,241,50,179,460,77,3..., dimensions={0} | all-to-all | bytes 1048576 | tf_op jit(solution)/shard_map/all_to_all | solution.py:191
  35.0 2.2 %shard_map.69 = (f32[8,128]{1,0:T(8,128)}, f32[8,128]{1,0:T(8,128)}) custom-call(bf16[256,1024]{1,0:T(8,128)(2,1)S(1)} %bitcast.4, f32[8,128]{1,0:T(8,128)S(1)} %get-tuple-element.5.own_ref), custom_call_target="tpu_custom_call" | custom-call | tf_op jit(solution)/shard_map/pallas_call | solution.py:177

commit v9 on v8

--- a/solution.py
+++ b/solution.py
@@ -22,7 +22,7 @@
 
 def groups():
     out = []
-    for first_y, order in ((2, (2, 3, 0, 1)), (6, (0, 1, 2, 3))):
+    for first_y, order in ((2, (2, 3, 1, 0)), (6, (0, 1, 3, 2))):
         for x0 in range(4):
             for core0 in range(2):
                 members = [
@@ -119,7 +119,7 @@
     y_high, y_low = lax.rem(lax.axis_index("val") // 2, 2), lax.rem(lax.axis_index("cond"), 4)
     middle = (y_high == 0) == (y_low >= 2)
     last = got_ref[224:256, NPTS:].astype(jnp.float32)
-    head = jnp.where(middle, last[0:16], last[16:32])
+    head = jnp.where(middle, last[0:8], last[24:32])
 
     def own(values):
         return jnp.sum(jnp.where(mine, values, 0.0), axis=1, keepdims=True)

time: 37.4 us -> 37.1 us (level)
  no operation moved by 1% of the time
where the time goes in v9:
time: 37.1 us; the launch traced here: 36.9 us
  blocking collectives  33.2 us (89%)
  Pallas kernels  3.07 us (8%)
  between operations  0.64 us (2%)
    all_to_all x1, blocking collectives, per_device(): lax.all_to_all(sent, ('val', 'cond'), 0, 0, tiled=True, axis_index_groups...  33.2 us
    pallas_call x1, Pallas kernels, chi(): pl.pallas_call(functools.partial(chi_kernel, factor), out_shape=[jax.Shap...  2.19 us
    pallas_call x1, Pallas kernels, pack(): pl.pallas_call(pack_kernel, out_shape=[pltpu.VMEM((32, 8, 1024), jnp.bflo...  0.88 us

profile of v9, /device:TPU:1, one launch (start us, length us, event | category | flops | bytes accessed | tf_op | source)
XLA Modules:
  0.0 36.9 jit_solution(10765799846029469425)
XLA Ops:
  0.6 0.9 %shard_map.68 = (bf16[32,8,1024]{2,1,0:T(8,128)(2,1)S(1)}, f32[8,128]{1,0:T(8,128)S(1)}) custom-call(bf16[4,768]{1,0:T(4,128)(2,1)} %val_ref.1, bf16[8,768]{1,0:T(8,128)(2,1)} %cond_ref.1, bf16[1,4]{1,0:T(2,128)(2,1)} %bitcast.5, bf16[1,8]{1,0:T(2,128)(2,1)} %bitcast.6, s32[1,128]{1,0:T(1,128)} %bitcast.7), custom_call_target="tpu_custom_call" | custom-call | tf_op jit(solution)/shard_map/pallas_call | solution.py:168
  1.5 33.2 %all_to_all.5 = bf16[32,8,1024]{2,1,0:T(8,128)(2,1)S(1)} all-to-all(bf16[32,8,1024]{2,1,0:T(8,128)(2,1)S(1)} %get-tuple-element.4), channel_id=1, replica_groups={{508,125,63,446,376,505,443,314,244,373,311,182,112,241,179,50,460,77,1..., dimensions={0} | all-to-all | bytes 1048576 | tf_op jit(solution)/shard_map/all_to_all | solution.py:191
  34.7 2.2 %shard_map.69 = (f32[8,128]{1,0:T(8,128)}, f32[8,128]{1,0:T(8,128)}) custom-call(bf16[256,1024]{1,0:T(8,128)(2,1)S(1)} %bitcast.4, f32[8,128]{1,0:T(8,128)S(1)} %get-tuple-element.5.own_ref), custom_call_target="tpu_custom_call" | custom-call | tf_op jit(solution)/shard_map/pallas_call | solution.py:177
